TPU v7x, 32 devices: a whole 2x2x4 slice. The times are simulated.
32 devices in a mesh: group: 2 (over x), expert: 16 (over z, y, core).
Axes of the slice: x: 2, y: 2, z: 4, core: 2. Of those that a mesh axis runs over, the one named last changes fastest.
Arguments:
- q_latent: bfloat16 [2048, 16384], P(('group', 'expert')), parts along dimension 0
- q_rope: bfloat16 [2048, 4096], P(('group', 'expert')), parts along dimension 0, may hold values from -4 to 4
- latents: bfloat16 [2048, 256], P(('group', 'expert')), parts along dimension 0
- k_rope: bfloat16 [2048, 64], P(('group', 'expert')), parts along dimension 0, may hold values from -6 to 6
- moe_tokens: bfloat16 [512, 3584], P(('group', 'expert')), parts along dimension 0, may hold values from -6 to 6
- routes: int32 [512, 8], P(('group', 'expert')), parts along dimension 0, may hold values from 0 to 15, all different within a row; in each aligned block of 16 rows (0 to 15, 16 to 31, ...) at most 10 rows name the same one
- route_weights: float32 [512, 8], P(('group', 'expert')), parts along dimension 0, may hold values from 0.2 to 1
- w_gate: bfloat16 [16, 3584, 1024], P('expert'), may hold values from -0.09375 to 0.09375
- w_up: bfloat16 [16, 3584, 1024], P('expert'), may hold values from -0.09375 to 0.09375
- w_down: bfloat16 [16, 1024, 3584], P('expert'), may hold values from -0.1875 to 0.1875
Outputs:
- attention_out: bfloat16 [2048, 16384], P(('group', 'expert')), parts along dimension 0
- moe_out: bfloat16 [512, 3584], P(('group', 'expert')), parts along dimension 0
There are 2 independent parts, one for each index of `group`. A program takes and returns all parts, laid end to end along the dimension named above; an argument that names none is the same for every part. Nothing has to cross between parts.
Inputs may be any that keep to these rules, and one draw needn't show every extreme that they name: `routes`: each row names 8 different experts; in each aligned block of 16 rows (the rows of one device) no expert is named by more than 10 rows, a bound that some block reaches.
All inputs are finite; a program needn't handle non-finite values.
Results may differ from a plain program's by a relative error of at most 0.0058.
Values may be sent and summed in bfloat16 or wider, within the bound.
A program may use at most 128 MiB of HBM per device.

v0:
```python
import math

import jax
import jax.numpy as jnp
from jax import lax
from jax.sharding import PartitionSpec as P

LATENT = 256
ROPE_DIM = 64
EXPERTS = 16


SCORE_SCALE = 192.0 ** (-0.5)
MASKED = -1e30


def expert_ffn(token_rows, gate_matrix, up_matrix, down_matrix):
    gate_part = jnp.dot(token_rows, gate_matrix, preferred_element_type=jnp.float32)
    up_part = jnp.dot(token_rows, up_matrix, preferred_element_type=jnp.float32)
    hidden_rows = (jax.nn.silu(gate_part) * up_part).astype(jnp.bfloat16)
    return jnp.dot(hidden_rows, down_matrix, preferred_element_type=jnp.float32).astype(
        jnp.bfloat16
    )


def per_device(
    q_latent, q_rope, latents, k_rope, moe_tokens, routes, route_weights, w_gate, w_up, w_down
):
    query_count = q_latent.shape[0]
    head_count = q_rope.shape[1] // ROPE_DIM
    device_index = lax.axis_index("expert")
    query_first = device_index * query_count
    query_lat = q_latent.reshape(query_count, head_count, LATENT)
    query_rope = q_rope.reshape(query_count, head_count, ROPE_DIM)
    query_pos = query_first + jnp.arange(query_count, dtype=jnp.int32)
    query_last = query_first + query_count - 1

    def tile_update(state_now, lat_keys, rope_keys, first_key):
        running, totals, accumulated = state_now
        key_count = lat_keys.shape[0]
        scores = jnp.einsum("qhl,kl->qhk", query_lat, lat_keys, preferred_element_type=jnp.float32)
        scores = scores + jnp.einsum(
            "qhe,ke->qhk", query_rope, rope_keys, preferred_element_type=jnp.float32
        )
        scores = scores * SCORE_SCALE
        key_pos = first_key + jnp.arange(key_count, dtype=jnp.int32)
        visible = (key_pos[None, :] <= query_pos[:, None])[:, None, :]
        scores = jnp.where(visible, scores, MASKED)
        new_peak = jnp.maximum(running, jnp.max(scores, axis=2))
        weights_exp = jnp.where(visible, jnp.exp(scores - new_peak[:, :, None]), 0.0)
        factor = jnp.exp(running - new_peak)
        totals = totals * factor + jnp.sum(weights_exp, axis=2)
        accumulated = accumulated * factor[:, :, None] + jnp.einsum(
            "qhk,kl->qhl",
            weights_exp.astype(jnp.bfloat16),
            lat_keys,
            preferred_element_type=jnp.float32,
        )
        return (new_peak, totals, accumulated)

    initial = (
        jnp.full((query_count, head_count), MASKED, jnp.float32),
        jnp.zeros((query_count, head_count), jnp.float32),
        jnp.zeros((query_count, head_count, LATENT), jnp.float32),
    )
    lat_whole, rope_whole = (
        lax.all_gather(latents, "expert", axis=0, tiled=True),
        lax.all_gather(k_rope, "expert", axis=0, tiled=True),
    )
    whole_keys = lat_whole.shape[0]
    block_keys = math.gcd(whole_keys, 512)

    def whole_step(block_number, fold_state):
        offset = (block_number * block_keys).astype(jnp.int32)
        lat_keys = lax.dynamic_slice_in_dim(lat_whole, offset, block_keys, 0)
        rope_keys = lax.dynamic_slice_in_dim(rope_whole, offset, block_keys, 0)
        return tile_update(fold_state, lat_keys, rope_keys, offset)

    block_stop = query_last // block_keys + 1
    running, totals, accumulated = lax.fori_loop(0, block_stop, whole_step, initial)
    attention_out = (
        (accumulated / totals[:, :, None])
        .astype(jnp.bfloat16)
        .reshape(query_count, head_count * LATENT)
    )
    token_count, top_count = routes.shape
    row_width = moe_tokens.shape[1]
    device_count = lax.axis_size("expert")
    expert_count = EXPERTS
    split_count = device_count // expert_count
    capacity = 5 * token_count * top_count // (4 * expert_count)
    flat_routes = routes.reshape(token_count * top_count)
    onehot_routes = (
        flat_routes[:, None] == jnp.arange(expert_count, dtype=jnp.int32)[None, :]
    ).astype(jnp.int32)
    earlier_rows = jnp.cumsum(onehot_routes, axis=0) - onehot_routes
    slot_index = jnp.sum(earlier_rows * onehot_routes, axis=1)
    target_row = flat_routes * capacity + slot_index
    per_expert = jnp.zeros((expert_count * capacity, row_width), jnp.bfloat16)
    per_expert = per_expert.at[target_row].set(jnp.repeat(moe_tokens, top_count, axis=0))
    per_expert = per_expert.reshape(expert_count, 1, capacity, row_width)
    outgoing = jnp.broadcast_to(per_expert, (expert_count, split_count, capacity, row_width))
    outgoing = outgoing.reshape(device_count, capacity, row_width)
    gate_matrix = w_gate[0]
    up_matrix = w_up[0]
    down_matrix = w_down[0]
    batch_rows = lax.all_to_all(outgoing, "expert", split_axis=0, concat_axis=0, tiled=True)
    source_count, item_count, width_now = batch_rows.shape
    flat_out = expert_ffn(
        batch_rows.reshape(source_count * item_count, width_now),
        gate_matrix,
        up_matrix,
        down_matrix,
    )
    produced = flat_out.reshape(source_count, item_count, width_now)
    returned = lax.all_to_all(produced, "expert", split_axis=0, concat_axis=0, tiled=True)
    returned = returned.reshape(expert_count, split_count, capacity, row_width)
    picked = returned[flat_routes, :, slot_index]
    picked = picked.reshape(token_count, top_count, split_count, row_width)
    weighted = picked.astype(jnp.float32) * route_weights[:, :, None, None]
    moe_out = jnp.sum(weighted, axis=(1, 2)).astype(jnp.bfloat16)
    return (attention_out, moe_out)


def solution(mesh):
    in_specs = (
        P(("group", "expert"), None),
        P(("group", "expert"), None),
        P(("group", "expert"), None),
        P(("group", "expert"), None),
        P(("group", "expert"), None),
        P(("group", "expert"), None),
        P(("group", "expert"), None),
        P("expert", None, None),
        P("expert", None, None),
        P("expert", None, None),
    )
    out_specs = (P(("group", "expert"), None), P(("group", "expert"), None))
    return jax.shard_map(
        per_device, mesh=mesh, in_specs=in_specs, out_specs=out_specs, check_vma=False
    )
```

profile of v0, /device:TPU:15, one launch (start us, length us, event | category | flops | bytes accessed | tf_op | source)
XLA Modules:
  0.0 163.7 jit_solution(4598349161501757067)
XLA Ops:
  0.6 0.0 copy-start
  0.6 0.8 copy.23
  1.4 0.1 eq.15
  1.5 0.1 reshape.155
  1.6 0.1 fusion.45
  1.7 0.2 reduce_window_sum.11
  1.9 0.2 select_reduce_fusion
  2.1 0.0 copy-done
  2.1 2.2 %scatter_custom_fusion = bf16[160,3584]{1,0:T(8,128)(2,1)S(1)} fusion(s32[128]{0:T(128)S(1)} %get-tuple-element.117, bf16[]{:T(256)} %constant.60.clone.1, bf16[16,3584]{1,0:T(8,128)(2,1)S(1)} %copy-done), kind=kCustom, calls=%fused_computation.40 | custom fusion | bytes 1261570 | tf_op jit(solution)/shard_map/scatter | solution.py:100
  4.3 1.4 reshape_reshape.3
  5.7 0.0 copy-start.6
  5.7 0.0 copy-start.5
  5.7 6.7 %all-to-all-start = ((bf16[16,10,3584]{2,1,0:T(8,128)(2,1)}), bf16[16,10,3584]{2,1,0:T(8,128)(2,1)}, u32[]{:S(2)}, u32[]{:S(2)}) async-start(bf16[16,10,3584]{2,1,0:T(8,128)(2,1)} %reshape_reshape.3), calls=%async_computation | async-start | bytes 3670016 | tf_op jit(solution)/shard_map/all_to_all | solution.py:107
  12.4 2.1 %copy.27 = bf16[8,8,64,256]{3,2,1,0:T(8,128)(2,1)S(1)} copy(bf16[8,8,64,256]{3,1,2,0:T(8,128)(2,1)} %bitcast.66) | data formatting | bytes 4194304
  14.5 2.1 %reshape.153 = bf16[64,64,64]{2,1,0:T(8,128)(2,1)S(1)} reshape(bf16[64,4096]{1,0:T(8,128)(2,1)} %param.13) | data formatting | bytes 1048576 | tf_op jit(solution)/shard_map/reshape | solution.py:34
  16.6 0.0 copy-done.6
  16.6 49.3 %all_gather.7 = bf16[1024,64]{1,0:T(8,128)(2,1)} all-gather(bf16[64,64]{1,0:T(8,128)(2,1)S(1)} %copy-done.6), channel_id=1, replica_groups=mesh['group'=2,'expert'=16] {'expert'}, dimensions={0}, use_global_device_ids=true | all-gather | bytes 139264 | tf_op jit(solution)/shard_map/all_gather | solution.py:68
  66.0 1.1 copy.22
  67.0 0.0 copy-done.5
  67.0 18.3 %all_gather.6 = bf16[1024,256]{1,0:T(8,128)(2,1)} all-gather(bf16[64,256]{1,0:T(8,128)(2,1)S(1)} %copy-done.5), channel_id=1, replica_groups=mesh['group'=2,'expert'=16] {'expert'}, dimensions={0}, use_global_device_ids=true | all-gather | bytes 557056 | tf_op jit(solution)/shard_map/all_gather | solution.py:67
  85.3 0.0 all-to-all-done
  85.3 2.5 %reshape.157 = bf16[160,3584]{1,0:T(8,128)(2,1)} reshape(bf16[16,10,3584]{2,1,0:T(8,128)(2,1)} %all-to-all-done) | data formatting | bytes 2293760 | tf_op jit(solution)/shard_map/reshape | solution.py:110
  87.8 5.7 %fusion.26 = f32[160,1024]{1,0:T(8,128)} fusion(bf16[160,3584]{1,0:T(8,128)(2,1)} %reshape.157, bf16[1,3584,1024]{2,1,0:T(8,128)(2,1)} %param.19), kind=kOutput, calls=%fused_computation.32 | convolution fusion | flops 1174405120 | bytes 9142272 | tf_op jit(solution)/shard_map/dot_general | solution.py:18
  93.4 9.3 %fusion.28 = bf16[160,3584]{1,0:T(8,128)(2,1)} fusion(bf16[1,1024,3584]{2,1,0:T(8,128)(2,1)} %param.21, bf16[160,3584]{1,0:T(8,128)(2,1)} %reshape.157, bf16[1,3584,1024]{2,1,0:T(8,128)(2,1)} %param.20, f32[160,1024]{1,0:T(8,128)} %fusion.26), kind=kOutput, calls=%fused_computation.34 | convolution fusion | flops 2350366720 | bytes 17629184 | tf_op jit(solution)/shard_map/dot_general | solution.py:21
  102.7 2.5 %reshape.158 = bf16[16,10,3584]{2,1,0:T(8,128)(2,1)} reshape(bf16[160,3584]{1,0:T(8,128)(2,1)} %fusion.28) | data formatting | bytes 2293760 | tf_op jit(solution)/shard_map/reshape | solution.py:115
  105.2 9.5 %all-to-all-start.1 = ((bf16[16,10,3584]{2,1,0:T(8,128)(2,1)}), bf16[16,10,3584]{2,1,0:T(8,128)(2,1)}, u32[]{:S(2)}, u32[]{:S(2)}) async-start(bf16[16,10,3584]{2,1,0:T(8,128)(2,1)} %reshape.158), calls=%async_computation.1 | async-start | bytes 3670016 | tf_op jit(solution)/shard_map/all_to_all | solution.py:116
  114.8 2.4 %broadcast_in_dim.46 = f32[64,64,256]{2,1,0:T(8,128)} broadcast(f32[]{:T(128)} %constant.35.clone.1), dimensions={} | broadcast | bytes 4194308 | tf_op jit(solution)/shard_map/broadcast_in_dim | solution.py:64
  117.2 11.6 %while.15 = (s32[]{:T(128)}, f32[64,64]{1,0:T(8,128)S(1)}, f32[64,64]{1,0:T(8,128)S(1)}, f32[64,64,256]{2,1,0:T(8,128)}, s32[]{:T(128)}, /*index=5*/bf16[1024,25...) while((s32[]{:T(128)}, f32[64,64]{1,0:T(8,128)S(1)}, ...), condition=%wide.region_3.4_spmd.clone, body=%wide.region_0.3_spmd.clone.sunk | while | flops 2439029248 | bytes 90149648 | solution.py:80
  117.2 2.2 %fusion.72 = f32[512,64,64]{0,2,1:T(8,128)S(1)} fusion(bf16[64,64,256]{2,1,0:T(8,128)(2,1)S(1)} %get-tuple-element.222, bf16[1024,256]{1,0:T(8,128)(2,1)} %get-tuple-element.221, s32[]{:T(128)S(6)} %select_n.88), kind=kOutput, calls=%fused_computation.13.clone.1 | convolution fusion | flops 1073741824 | bytes 10747908 | tf_op jit(solution)/shard_map/while/body/qhl,kl->qhk/dot_general | solution.py:41
  119.5 0.1 broadcast_compare_fusion.2
  119.6 1.6 fusion.73
  121.2 0.0 copy-start.2
  121.2 0.0 copy-start.4
  121.2 2.5 %fusion.74 = f32[64,64]{1,0:T(8,128)S(1)} fusion(f32[64,64,512]{2,1,0:T(8,128)S(1)} %get-tuple-element.185, f32[64,64]{1,0:T(8,128)S(1)} %max.5, pred[64,512]{1,0:T(8,128)(4,1)S(1)} %broadcast_compare_fusion.2), kind=kLoop, calls=%fused_computation.6.clone.1 | loop fusion | flops 6287360 | bytes 8454144 | tf_op jit(solution)/shard_map/while/body/reduce_sum | solution.py:52
  123.8 0.0 copy-done.2
  123.8 0.0 copy-done.4
  123.8 3.1 %multiply_add_fusion.5 = f32[64,64,256]{2,1,0:T(8,128)S(1)} fusion(f32[64,64,256]{2,1,0:T(8,128)S(1)} %copy-done.2, f32[64,64]{1,0:T(8,128)S(1)} %get-tuple-element.187, f32[64,64,512]{2,1,0:T(8,128)S(1)} %get-tuple-element.185, f32[64,64]{1,0:T(8,128)S(1)} %max.5, pred[64,512]{1,0:T(8,128)(4,1)S(1)} %broadcast_compare_fusion.2, ...), kind=kOutput, calls=%fused_computation.8.clone.1 | convolution fusion | flops 1082130432 | bytes 17137668 | tf_op jit(solution)/shard_map/while/body/qhk,kl->qhl/dot_general | solution.py:53
  126.8 0.0 copy-start.3
  126.9 1.9 %copy-done.3 = f32[64,64,256]{2,1,0:T(8,128)} copy-done((f32[64,64,256]{2,1,0:T(8,128)}, f32[64,64,256]{2,1,0:T(8,128)S(1)}, u32[]{:S(2)}) %copy-start.3) | copy-done | bytes 4194328 | tf_op jit(solution)/shard_map/while
  128.8 0.0 copy-start.7
  128.8 2.6 %divide_convert_fusion = bf16[64,64,256]{2,1,0:T(8,128)(2,1)S(1)} fusion(f32[64,64,256]{2,1,0:T(8,128)} %get-tuple-element.56, f32[64,64]{1,0:T(8,128)S(1)} %get-tuple-element.57), kind=kLoop, calls=%fused_computation.35 | loop fusion | flops 2097152 | bytes 6307840 | tf_op jit(solution)/shard_map/convert_element_type | solution.py:83
  131.4 2.6 %copy.28 = bf16[8,8,64,256]{3,1,2,0:T(8,128)(2,1)} copy(bf16[8,8,64,256]{3,2,1,0:T(8,128)(2,1)S(1)} %bitcast.65) | data formatting | bytes 4194304
  134.0 0.0 copy-done.7
  134.0 0.1 copy.26
  134.1 22.6 %all-to-all-done.1 = bf16[16,10,3584]{2,1,0:T(8,128)(2,1)} async-done(((bf16[16,10,3584]{2,1,0:T(8,128)(2,1)}), bf16[16,10,3584]{2,1,0:T(8,128)(2,1)}, u32[]{:S(2)}, u32[]{:S(2)}) %all-to-all-start.1) | async-done | bytes 1146912 | tf_op jit(solution)/shard_map/all_to_all | solution.py:116
  156.7 2.1 %copy.25 = bf16[16,10,3584]{2,0,1:T(8,128)(2,1)S(1)} copy(bf16[16,10,3584]{2,1,0:T(8,128)(2,1)} %all-to-all-done.1) | data formatting | bytes 2293760 | tf_op jit(solution)/shard_map/all_to_all | solution.py:116
  158.8 0.0 copy-start.1
  158.8 3.5 %gather_fusion = bf16[128,3584]{1,0:T(8,128)(2,1)S(1)} fusion(bf16[16,10,3584]{2,0,1:T(8,128)(2,1)S(1)} %copy.25, s32[128]{0:T(128)S(1)} %get-tuple-element.116), kind=kCustom, calls=%fused_computation | custom fusion | bytes 1836032 | tf_op jit(solution)/shard_map/gather | solution.py:118
  162.4 1.3 fusion.31
  163.7 0.0 copy-done.1
  (8 shorter events, 0.1 us)
Async XLA Ops:
  0.6 1.4 copy-start
  5.7 10.9 %copy-start.6 = (bf16[64,64]{1,0:T(8,128)(2,1)S(1)}, bf16[64,64]{1,0:T(8,128)(2,1)}, u32[]{:S(2)}) copy-start(bf16[64,64]{1,0:T(8,128)(2,1)} %param.15) | copy-start | bytes 24580
  5.7 61.3 %copy-start.5 = (bf16[64,256]{1,0:T(8,128)(2,1)S(1)}, bf16[64,256]{1,0:T(8,128)(2,1)}, u32[]{:S(2)}) copy-start(bf16[64,256]{1,0:T(8,128)(2,1)} %param.14) | copy-start | bytes 98308
  5.7 79.6 %all-to-all-start = ((bf16[16,10,3584]{2,1,0:T(8,128)(2,1)}), bf16[16,10,3584]{2,1,0:T(8,128)(2,1)}, u32[]{:S(2)}, u32[]{:S(2)}) async-start(bf16[16,10,3584]{2,1,0:T(8,128)(2,1)} %reshape_reshape.3), calls=%async_computation | async-start | bytes 3670016 | tf_op jit(solution)/shard_map/all_to_all | solution.py:107
  105.2 51.4 %all-to-all-start.1 = ((bf16[16,10,3584]{2,1,0:T(8,128)(2,1)}), bf16[16,10,3584]{2,1,0:T(8,128)(2,1)}, u32[]{:S(2)}, u32[]{:S(2)}) async-start(bf16[16,10,3584]{2,1,0:T(8,128)(2,1)} %reshape.158), calls=%async_computation.1 | async-start | bytes 3670016 | tf_op jit(solution)/shard_map/all_to_all | solution.py:116
  121.2 2.6 %copy-start.2 = (f32[64,64,256]{2,1,0:T(8,128)S(1)}, f32[64,64,256]{2,1,0:T(8,128)}, u32[]{:S(2)}) copy-start(f32[64,64,256]{2,1,0:T(8,128)} %get-tuple-element.205) | copy-start | bytes 12582916 | tf_op jit(solution)/shard_map/while
  121.2 2.6 %copy-start.4 = (bf16[1024,256]{1,0:T(8,128)(2,1)S(1)}, bf16[1024,256]{1,0:T(8,128)(2,1)}, u32[]{:S(2)}) copy-start(bf16[1024,256]{1,0:T(8,128)(2,1)} %get-tuple-element.221) | copy-start | bytes 1572868 | tf_op jit(solution)/shard_map/while
  126.8 1.9 %copy-start.3 = (f32[64,64,256]{2,1,0:T(8,128)}, f32[64,64,256]{2,1,0:T(8,128)S(1)}, u32[]{:S(2)}) copy-start(f32[64,64,256]{2,1,0:T(8,128)S(1)} %multiply_add_fusion.5) | copy-start | bytes 12582916 | tf_op jit(solution)/shard_map/while
  128.8 5.2 %copy-start.7 = (f32[16,8]{0,1:T(8,128)S(1)}, f32[16,8]{0,1:T(8,128)}, u32[]{:S(2)}) copy-start(f32[16,8]{0,1:T(8,128)} %param.18) | copy-start | bytes 1540
  158.8 4.9 %copy-start.1 = (bf16[16,3584]{1,0:T(8,128)(2,1)S(1)}, bf16[16,3584]{1,0:T(8,128)(2,1)}, u32[]{:S(2)}) copy-start(bf16[16,3584]{1,0:T(8,128)(2,1)} %param.16) | copy-start | bytes 344068
where the time goes:
time: 164 us
  blocking collectives  67.6 us (41%)
  local copies, waits for them, and re-layouts  27.6 us (17%)
  waiting for transfers between devices  22.6 us (14%)
  matrix products  21.9 us (13%)
  starting transfers between devices  16.2 us (10%)
  other arithmetic  7.02 us (4%)
    all_gather x1, blocking collectives, per_device(): lax.all_gather(k_rope, 'expert', axis=0, tiled=True)  49.3 us
    all_to_all x1, waiting for transfers between devices, per_device(): lax.all_to_all(produced, 'expert', split_axis=0, concat_axis=0, tiled=True)  22.6 us
    all_gather x1, blocking collectives, per_device(): lax.all_gather(latents, 'expert', axis=0, tiled=True)  18.3 us
    all_to_all x1, starting transfers between devices, per_device(): lax.all_to_all(produced, 'expert', split_axis=0, concat_axis=0, tiled=True)  9.52 us
    dot_general x1, matrix products, expert_ffn(): jnp.dot(hidden_rows, down_matrix, preferred_element_type=jnp.float32)  9.28 us
    unnamed x15, local copies, waits for them, and re-layouts  6.69 us
    all_to_all x1, starting transfers between devices, per_device(): lax.all_to_all(outgoing, 'expert', split_axis=0, concat_axis=0, tiled=True)  6.69 us
    dot_general x1, matrix products, expert_ffn(): jnp.dot(token_rows, gate_matrix, preferred_element_type=jnp.float32)  5.68 us
  transfers between devices with their start and end apart: 2, of which 1 were waited for; matrix products, arithmetic and copies ran while one was open for 14% of the time, Pallas kernels for 0%

commit v1 on v0

v1 whole, which is shorter than its diff:
```python
import functools

import jax
import jax.numpy as jnp
from jax import lax
from jax.experimental import pallas as pl
from jax.experimental.pallas import tpu as pltpu
from jax.sharding import PartitionSpec as P

LATENT = 256
ROPE_DIM = 64
EXPERTS = 16
LANES = 128

EXP_SCALE = 192.0 ** (-0.5) * 1.4426950408889634
MASKED = -1e30

SIDES = 2
CORES = 2
KEY_WIDTH = LATENT + LANES
PAIRS = 4
ROW_BLOCK = 256
CHUNKS = (1024, 1024, 1024, 512)
EARLY = 4


class Gather:
    def __init__(self, buffer, height, slot_of, device_of, send, recv):
        self.buffer, self.height, self.slot_of, self.device_of = buffer, height, slot_of, device_of
        self.send, self.recv = send, recv
        self.started = []

    def copy(self, place, target, index):
        slot = self.slot_of(*place)
        block = self.buffer.at[pl.ds(pl.multiple_of(slot * self.height, self.height), self.height)]
        return pltpu.make_async_remote_copy(
            src_ref=block,
            dst_ref=block,
            send_sem=self.send.at[index],
            recv_sem=self.recv.at[slot],
            device_id={"expert": self.device_of(*target)},
            device_id_type=pl.DeviceIdType.MESH,
        )

    def start(self, place, target):
        copy = self.copy(place, target, len(self.started))
        copy.start()
        self.started.append(copy)

    def arrive(self, place, target):
        self.copy(place, target, 0).wait_recv()

    def finish(self):
        for copy in self.started:
            copy.wait_send()


def kernel(
    n,
    split,
    q_lat,
    q_rope,
    latents,
    k_rope,
    tokens,
    routes,
    route_weights,
    w_gate,
    w_up,
    w_down,
    att_out,
    moe_out,
    keys,
    toks,
    part,
    from_core,
    from_side,
    from_line,
    kt_even,
    kt_odd,
    hidden,
    gate,
    up,
    down,
    weight_sem,
    keys_send,
    keys_recv,
    toks_send,
    toks_recv,
    core_send,
    core_recv,
    side_send,
    side_recv,
    line_send,
    line_recv,
):
    count = n // (SIDES * CORES)
    queries = q_lat.shape[0]
    token_count, width = tokens.shape
    f_dev = gate.shape[1]
    all_keys = keys.shape[0]
    all_tokens = toks.shape[0]
    me = lax.axis_index("expert")
    core, side, line = me % CORES, (me // CORES) % SIDES, me // (SIDES * CORES)
    mine = (line, side, core)
    sibling = (line, side, 1 - core)
    across = (line, 1 - side, core)
    if count == 4:
        others = [line + 1 - 2 * (line % 2), (line + 2) % 4, 3 - line]
    else:
        others = [(line + k) % count for k in range(1, count)]

    def device_of(line, side, core):
        return (line * SIDES + side) * CORES + core

    def token_slot(line, side, core):
        return (core * SIDES + side) * count + line

    weight_copies = [
        pltpu.make_async_copy(w_gate.at[0], gate, weight_sem.at[0]),
        pltpu.make_async_copy(w_up.at[0], up, weight_sem.at[1]),
        pltpu.make_async_copy(w_down.at[0], down, weight_sem.at[2]),
    ]
    for copy in weight_copies:
        copy.start()

    barrier = pltpu.get_barrier_semaphore()
    partners = [sibling, across] + [(other, side, core) for other in others]
    for partner in partners:
        pl.semaphore_signal(
            barrier,
            inc=1,
            device_id={"expert": device_of(*partner)},
            device_id_type=pl.DeviceIdType.MESH,
        )

    key_rows = pl.ds(pl.multiple_of(me * queries, queries), queries)
    keys[key_rows, :LATENT] = latents[...]
    keys[key_rows, LATENT:] = jnp.concatenate(
        [k_rope[...], jnp.zeros((queries, LANES - ROPE_DIM), jnp.bfloat16)], axis=1
    )
    my_token_slot = token_slot(*mine)
    token_rows = pl.ds(pl.multiple_of(my_token_slot * token_count, token_count), token_count)
    toks[token_rows, :width] = tokens[...]
    lane = lax.broadcasted_iota(jnp.int32, (token_count, LANES), 1)
    dense = jnp.zeros((token_count, LANES), jnp.float32)
    for k in range(routes.shape[1]):
        dense = dense + jnp.where(routes[:, k : k + 1] == lane, route_weights[:, k : k + 1], 0.0)
    dense_high = dense.astype(jnp.bfloat16)
    dense_low = (dense - dense_high.astype(jnp.float32)).astype(jnp.bfloat16)
    toks[token_rows, width : width + LANES] = dense_high
    toks[token_rows, width + LANES :] = dense_low

    pl.semaphore_wait(barrier, len(partners))

    key_gather = Gather(keys, queries, device_of, device_of, keys_send, keys_recv)
    tok_gather = Gather(toks, token_count, token_slot, device_of, toks_send, toks_recv)
    for gather in (key_gather, tok_gather):
        gather.start(mine, across)
        for other in others:
            gather.start(mine, (other, side, core))
        gather.start(mine, sibling)

    def forward_line(gather, other):
        place = (other, side, core)
        gather.arrive(place, sibling)
        gather.start(place, across)
        gather.start(place, sibling)

    def forward_side(gather, other):
        place = (other, 1 - side, core)
        gather.arrive(place, sibling)
        gather.start(place, sibling)

    def last_arrivals(gather):
        for other in [line] + others:
            for s in range(SIDES):
                gather.arrive((other, s, 1 - core), sibling)

    for other in others:
        forward_line(key_gather, other)
    for other in [line] + others:
        forward_side(key_gather, other)
    last_arrivals(key_gather)

    first = me * queries
    zero_rows = jnp.zeros((ROPE_DIM, ROW_BLOCK), jnp.bfloat16)
    for start in range(0, all_keys, ROW_BLOCK):
        cols = slice(start, start + ROW_BLOCK)
        turned = jnp.transpose(keys[cols, :])
        kt_even[:KEY_WIDTH, cols] = turned
        kt_odd[:LATENT, cols] = turned[:LATENT]
        kt_odd[LATENT : LATENT + ROPE_DIM, cols] = zero_rows
        kt_odd[LATENT + ROPE_DIM : KEY_WIDTH, cols] = turned[LATENT : LATENT + ROPE_DIM]
        row = lax.broadcasted_iota(jnp.int32, (LANES, ROW_BLOCK), 0)
        key = lax.broadcasted_iota(jnp.int32, (LANES, ROW_BLOCK), 1) + start
        mask = jnp.where(key > first + row, MASKED, 0.0).astype(jnp.bfloat16)
        kt_even[KEY_WIDTH:, cols] = mask
        kt_odd[KEY_WIDTH:, cols] = mask

    picks = jnp.where(
        lax.broadcasted_iota(jnp.int32, (queries, LANES), 0)
        == lax.broadcasted_iota(jnp.int32, (queries, LANES), 1),
        1.0,
        0.0,
    ).astype(jnp.bfloat16)

    def attend(step, carry):
        for odd, kt in ((0, kt_even), (1, kt_odd)):
            rows = []
            heads = []
            for p in range(PAIRS):
                pair = step * PAIRS + p
                head = pl.ds(pl.multiple_of((2 * pair + odd) * LATENT, LATENT), LATENT)
                ropes = pl.ds(pl.multiple_of(pair * LANES, LANES), LANES)
                heads.append(head)
                rows.append(jnp.concatenate([q_lat[:, head], q_rope[:, ropes], picks], axis=1))
            scores = jnp.dot(
                jnp.concatenate(rows, axis=0), kt[...], preferred_element_type=jnp.float32
            )
            peak = jnp.max(scores, axis=1, keepdims=True)
            weights = jnp.exp2((scores - peak) * EXP_SCALE)
            totals = jnp.sum(weights, axis=1, keepdims=True)
            mixed = jnp.dot(
                weights.astype(jnp.bfloat16),
                keys[:, :LATENT],
                preferred_element_type=jnp.float32,
            )
            mixed = (mixed / totals).astype(jnp.bfloat16)
            for p in range(PAIRS):
                att_out[:, heads[p]] = mixed[p * queries : (p + 1) * queries]
        return carry

    steps = q_lat.shape[1] // (2 * PAIRS * LATENT)

    def attend_some(low, high):
        lax.fori_loop(low, high, attend, 0)

    early = min(EARLY, steps)
    for at, other in enumerate(others):
        if at < early:
            attend_some(at, at + 1)
        forward_line(tok_gather, other)
    done = min(len(others), early)
    attend_some(done, early)
    for other in [line] + others:
        forward_side(tok_gather, other)
    last_arrivals(tok_gather)
    weight_copies[0].wait()
    weight_copies[1].wait()

    expert = me // split
    blocks = all_tokens // ROW_BLOCK

    def gate_up(at, carry):
        rows = pl.ds(pl.multiple_of((at % blocks) * ROW_BLOCK, ROW_BLOCK), ROW_BLOCK)
        cols = pl.ds(pl.multiple_of((at // blocks) * 256, 256), 256)
        x = toks[rows, :width]
        g = jnp.dot(x, gate[:, cols], preferred_element_type=jnp.float32)
        u = jnp.dot(x, up[:, cols], preferred_element_type=jnp.float32)
        hidden[rows, cols] = (g / (1.0 + jnp.exp(-g)) * u).astype(jnp.bfloat16)
        return carry

    lax.fori_loop(0, blocks * (f_dev // 256), gate_up, 0)
    weight_copies[2].wait()

    half, quarter = all_tokens // 2, all_tokens // 4
    near_half = pl.ds(pl.multiple_of(core * half, half), half)
    far_half = pl.ds(pl.multiple_of((1 - core) * half, half), half)
    near_quarter = pl.ds(pl.multiple_of(core * half + side * quarter, quarter), quarter)
    far_quarter = pl.ds(pl.multiple_of(core * half + (1 - side) * quarter, quarter), quarter)
    spans = []
    at = 0
    for size in CHUNKS:
        spans.append(slice(at, at + size))
        at += size
    started = []

    def remote(src, dst, send, recv, target):
        return pltpu.make_async_remote_copy(
            src_ref=src,
            dst_ref=dst,
            send_sem=send,
            recv_sem=recv,
            device_id={"expert": device_of(*target)},
            device_id_type=pl.DeviceIdType.MESH,
        )

    def core_copy(j):
        return remote(
            part.at[far_half, spans[j]],
            from_core.at[:, spans[j]],
            core_send.at[j],
            core_recv.at[j],
            sibling,
        )

    def side_copy(j):
        return remote(
            part.at[far_quarter, spans[j]],
            from_side.at[:, spans[j]],
            side_send.at[j],
            side_recv.at[j],
            across,
        )

    def line_rows(line):
        slot = token_slot(line, side, core)
        return pl.ds(pl.multiple_of(slot * token_count, token_count), token_count)

    def line_slot(line):
        return pl.ds(pl.multiple_of(line * token_count, token_count), token_count)

    def line_copy(j, k, owner):
        return remote(
            part.at[line_rows(others[k]), spans[j]],
            from_line.at[line_slot(owner), spans[j]],
            line_send.at[j * len(others) + k],
            line_recv.at[j * count + owner],
            (others[k], side, core),
        )

    def begin(copy):
        copy.start()
        started.append(copy)

    def produce(j):
        def one(at, carry):
            rows = pl.ds(pl.multiple_of(at * ROW_BLOCK, ROW_BLOCK), ROW_BLOCK)
            lanes = lax.broadcasted_iota(jnp.int32, (ROW_BLOCK, LANES), 1)
            both = toks[rows, width : width + LANES].astype(jnp.float32) + toks[
                rows, width + LANES :
            ].astype(jnp.float32)
            scale = jnp.sum(jnp.where(lanes == expert, both, 0.0), axis=1, keepdims=True)
            out = jnp.dot(hidden[rows, :], down[:, spans[j]], preferred_element_type=jnp.float32)
            part[rows, spans[j]] = (out * scale).astype(jnp.bfloat16)
            return carry

        lax.fori_loop(0, blocks, one, 0)
        begin(core_copy(j))

    def join_core(j):
        core_copy(j).wait_recv()
        summed = part[near_half, spans[j]].astype(jnp.float32) + from_core[:, spans[j]].astype(
            jnp.float32
        )
        part[near_half, spans[j]] = summed.astype(jnp.bfloat16)
        begin(side_copy(j))

    def join_side(j):
        side_copy(j).wait_recv()
        summed = part[near_quarter, spans[j]].astype(jnp.float32) + from_side[
            :, spans[j]
        ].astype(jnp.float32)
        part[near_quarter, spans[j]] = summed.astype(jnp.bfloat16)
        for k in range(len(others)):
            begin(line_copy(j, k, line))

    def join_line(j):
        summed = part[line_rows(line), spans[j]].astype(jnp.float32)
        for k, other in enumerate(others):
            line_copy(j, k, other).wait_recv()
            summed = summed + from_line[line_slot(other), spans[j]].astype(jnp.float32)
        moe_out[:, spans[j]] = summed.astype(jnp.bfloat16)

    parts = len(spans)
    for j in range(parts):
        produce(j)
        if j:
            join_core(j - 1)
    join_core(parts - 1)
    left = steps - early
    for j in range(parts):
        attend_some(early + left * j // parts, early + left * (j + 1) // parts)
        join_side(j)
    for j in range(parts):
        join_line(j)
    key_gather.finish()
    tok_gather.finish()
    for copy in started:
        copy.wait_send()


def per_device(
    q_latent, q_rope, latents, k_rope, moe_tokens, routes, route_weights, w_gate, w_up, w_down
):
    n = lax.axis_size("expert")
    queries = latents.shape[0]
    token_count, width = moe_tokens.shape
    f_dev = w_gate.shape[2]
    count = n // (SIDES * CORES)
    all_tokens = n * token_count
    vmem = pl.BlockSpec(memory_space=pltpu.VMEM)
    hbm = pl.BlockSpec(memory_space=pl.ANY)
    bf16 = jnp.bfloat16
    parts = len(CHUNKS)
    dma = pltpu.SemaphoreType.DMA
    return pl.pallas_call(
        functools.partial(kernel, n, n // EXPERTS),
        out_shape=(
            jax.ShapeDtypeStruct(q_latent.shape, bf16),
            jax.ShapeDtypeStruct(moe_tokens.shape, bf16),
        ),
        in_specs=[vmem] * 7 + [hbm] * 3,
        out_specs=(vmem, vmem),
        scratch_shapes=[
            pltpu.VMEM((n * queries, KEY_WIDTH), bf16),
            pltpu.VMEM((all_tokens, width + 2 * LANES), bf16),
            pltpu.VMEM((all_tokens, width), bf16),
            pltpu.VMEM((all_tokens // 2, width), bf16),
            pltpu.VMEM((all_tokens // 4, width), bf16),
            pltpu.VMEM((count * token_count, width), bf16),
            pltpu.VMEM((KEY_WIDTH + LANES, n * queries), bf16),
            pltpu.VMEM((KEY_WIDTH + LANES, n * queries), bf16),
            pltpu.VMEM((all_tokens, f_dev), bf16),
            pltpu.VMEM((width, f_dev), bf16),
            pltpu.VMEM((width, f_dev), bf16),
            pltpu.VMEM((f_dev, width), bf16),
            dma((3,)),
            dma((n - 1,)),
            dma((n,)),
            dma((n - 1,)),
            dma((n,)),
            dma((parts,)),
            dma((parts,)),
            dma((parts,)),
            dma((parts,)),
            dma((parts * (count - 1),)),
            dma((parts * count,)),
        ],
        compiler_params=pltpu.CompilerParams(
            collective_id=0, has_side_effects=True, vmem_limit_bytes=60 * 1024 * 1024
        ),
        cost_estimate=pl.CostEstimate(
            flops=2 * 4096 * 1024 * 768, bytes_accessed=30_000_000, transcendentals=4096 * 1024
        ),
    )(q_latent, q_rope, latents, k_rope, moe_tokens, routes, route_weights, w_gate, w_up, w_down)


def solution(mesh):
    rows = P(("group", "expert"), None)
    stacks = P("expert", None, None)
    return jax.shard_map(
        per_device,
        mesh=mesh,
        in_specs=(rows,) * 7 + (stacks,) * 3,
        out_specs=(rows, rows),
        check_vma=False,
    )
```

time: 164 us -> 64.7 us (0.39)
  the two profiles are of different devices: /device:TPU:15 before, /device:TPU:0 now
where the time goes in v1:
time: 64.7 us; the launch traced here: 64.5 us
  Pallas kernels  56.5 us (87%)
  local copies, waits for them, and re-layouts  7.31 us (11%)
    pallas_call x1, Pallas kernels, per_device(): pl.pallas_call(functools.partial(kernel, n, n // EXPERTS), out_shape=(jax...  56.5 us
    unnamed x4, local copies, waits for them, and re-layouts  7.31 us

profile of v1, /device:TPU:0, one launch (start us, length us, event | category | flops | bytes accessed | tf_op | source)
XLA Modules:
  0.0 64.5 jit_solution(17968625385345414710)
XLA Ops:
  0.6 1.4 %copy.12.routes = s32[16,8]{1,0:T(8,128)} copy(s32[16,8]{0,1:T(8,128)} %param.15) | data formatting | bytes 1024 | tf_op args[5]
  2.0 1.4 %copy.13.route_weights = f32[16,8]{1,0:T(8,128)} copy(f32[16,8]{0,1:T(8,128)} %param.16) | data formatting | bytes 1024 | tf_op args[6]
  3.3 56.5 %shard_map.113 = (bf16[64,16384]{1,0:T(8,128)(2,1)}, bf16[16,3584]{1,0:T(8,128)(2,1)}) custom-call(bf16[64,16384]{1,0:T(8,128)(2,1)} %q_lat.1, bf16[64,4096]{1,0:T(8,128)(2,1)} %q_rope.1, bf16[64,256]{1,0:T(8,128)(2,1)} %latents.1, bf16[64,64]{1,0:T(8,128)(2,1)} %k_rope.1, bf16[16,3584]{1,0:T(8,128)(2,1)} %tokens.1, s32[16,8]{1,0:T(8,128)} %copy.12.routes, ...), custom_call_target="tpu_custom_call" | custom-call | flops 6442450944 | bytes 30000000 | tf_op jit(solution)/shard_map/pallas_call | solution.py:398
  59.9 3.0 %copy.16 = bf16[64,16384]{1,0:T(8,128)(2,1)} copy(bf16[64,16384]{1,0:T(8,128)(2,1)} %get-tuple-element.4) | data formatting | bytes 4194304
  62.9 1.6 %copy.17 = bf16[16,3584]{1,0:T(8,128)(2,1)} copy(bf16[16,3584]{1,0:T(8,128)(2,1)} %get-tuple-element.5) | data formatting | bytes 229376

commit v2 on v1

--- a/solution.py
+++ b/solution.py
@@ -21,7 +21,6 @@
 PAIRS = 4
 ROW_BLOCK = 256
 CHUNKS = (1024, 1024, 1024, 512)
-EARLY = 4
 
 
 class Gather:
@@ -58,8 +57,8 @@
 def kernel(
     n,
     split,
-    q_lat,
-    q_rope,
+    q_lat_hbm,
+    q_rope_hbm,
     latents,
     k_rope,
     tokens,
@@ -82,6 +81,8 @@
     gate,
     up,
     down,
+    q_lat,
+    q_rope,
     weight_sem,
     keys_send,
     keys_recv,
@@ -121,7 +122,11 @@
         pltpu.make_async_copy(w_up.at[0], up, weight_sem.at[1]),
         pltpu.make_async_copy(w_down.at[0], down, weight_sem.at[2]),
     ]
-    for copy in weight_copies:
+    query_copies = [
+        pltpu.make_async_copy(q_lat_hbm, q_lat, weight_sem.at[3]),
+        pltpu.make_async_copy(q_rope_hbm, q_rope, weight_sem.at[4]),
+    ]
+    for copy in weight_copies + query_copies:
         copy.start()
 
     barrier = pltpu.get_barrier_semaphore()
@@ -144,8 +149,10 @@
     toks[token_rows, :width] = tokens[...]
     lane = lax.broadcasted_iota(jnp.int32, (token_count, LANES), 1)
     dense = jnp.zeros((token_count, LANES), jnp.float32)
-    for k in range(routes.shape[1]):
-        dense = dense + jnp.where(routes[:, k : k + 1] == lane, route_weights[:, k : k + 1], 0.0)
+    picked = jnp.transpose(routes[...])
+    amounts = jnp.transpose(route_weights[...])
+    for k in range(picked.shape[1]):
+        dense = dense + jnp.where(picked[:, k : k + 1] == lane, amounts[:, k : k + 1], 0.0)
     dense_high = dense.astype(jnp.bfloat16)
     dense_low = (dense - dense_high.astype(jnp.float32)).astype(jnp.bfloat16)
     toks[token_rows, width : width + LANES] = dense_high
@@ -155,7 +162,8 @@
 
     key_gather = Gather(keys, queries, device_of, device_of, keys_send, keys_recv)
     tok_gather = Gather(toks, token_count, token_slot, device_of, toks_send, toks_recv)
-    for gather in (key_gather, tok_gather):
+
+    def send_own(gather):
         gather.start(mine, across)
         for other in others:
             gather.start(mine, (other, side, core))
@@ -177,26 +185,15 @@
             for s in range(SIDES):
                 gather.arrive((other, s, 1 - core), sibling)
 
+    send_own(tok_gather)
     for other in others:
-        forward_line(key_gather, other)
+        forward_line(tok_gather, other)
+    send_own(key_gather)
     for other in [line] + others:
-        forward_side(key_gather, other)
-    last_arrivals(key_gather)
-
-    first = me * queries
-    zero_rows = jnp.zeros((ROPE_DIM, ROW_BLOCK), jnp.bfloat16)
-    for start in range(0, all_keys, ROW_BLOCK):
-        cols = slice(start, start + ROW_BLOCK)
-        turned = jnp.transpose(keys[cols, :])
-        kt_even[:KEY_WIDTH, cols] = turned
-        kt_odd[:LATENT, cols] = turned[:LATENT]
-        kt_odd[LATENT : LATENT + ROPE_DIM, cols] = zero_rows
-        kt_odd[LATENT + ROPE_DIM : KEY_WIDTH, cols] = turned[LATENT : LATENT + ROPE_DIM]
-        row = lax.broadcasted_iota(jnp.int32, (LANES, ROW_BLOCK), 0)
-        key = lax.broadcasted_iota(jnp.int32, (LANES, ROW_BLOCK), 1) + start
-        mask = jnp.where(key > first + row, MASKED, 0.0).astype(jnp.bfloat16)
-        kt_even[KEY_WIDTH:, cols] = mask
-        kt_odd[KEY_WIDTH:, cols] = mask
+        forward_side(tok_gather, other)
+    last_arrivals(tok_gather)
+    weight_copies[0].wait()
+    weight_copies[1].wait()
 
     picks = jnp.where(
         lax.broadcasted_iota(jnp.int32, (queries, LANES), 0)
@@ -236,19 +233,6 @@
     def attend_some(low, high):
         lax.fori_loop(low, high, attend, 0)
 
-    early = min(EARLY, steps)
-    for at, other in enumerate(others):
-        if at < early:
-            attend_some(at, at + 1)
-        forward_line(tok_gather, other)
-    done = min(len(others), early)
-    attend_some(done, early)
-    for other in [line] + others:
-        forward_side(tok_gather, other)
-    last_arrivals(tok_gather)
-    weight_copies[0].wait()
-    weight_copies[1].wait()
-
     expert = me // split
     blocks = all_tokens // ROW_BLOCK
 
@@ -261,7 +245,13 @@
         hidden[rows, cols] = (g / (1.0 + jnp.exp(-g)) * u).astype(jnp.bfloat16)
         return carry
 
-    lax.fori_loop(0, blocks * (f_dev // 256), gate_up, 0)
+    tiles = blocks * (f_dev // 256)
+    lax.fori_loop(0, tiles // 2, gate_up, 0)
+    for other in others:
+        forward_line(key_gather, other)
+    lax.fori_loop(tiles // 2, tiles, gate_up, 0)
+    for other in [line] + others:
+        forward_side(key_gather, other)
     weight_copies[2].wait()
 
     half, quarter = all_tokens // 2, all_tokens // 4
@@ -369,10 +359,29 @@
         if j:
             join_core(j - 1)
     join_core(parts - 1)
-    left = steps - early
+    last_arrivals(key_gather)
+    for copy in query_copies:
+        copy.wait()
+
+    first = me * queries
+    zero_rows = jnp.zeros((ROPE_DIM, ROW_BLOCK), jnp.bfloat16)
+    for start in range(0, all_keys, ROW_BLOCK):
+        cols = slice(start, start + ROW_BLOCK)
+        turned = jnp.transpose(keys[cols, :])
+        kt_even[:KEY_WIDTH, cols] = turned
+        kt_odd[:LATENT, cols] = turned[:LATENT]
+        kt_odd[LATENT : LATENT + ROPE_DIM, cols] = zero_rows
+        kt_odd[LATENT + ROPE_DIM : KEY_WIDTH, cols] = turned[LATENT : LATENT + ROPE_DIM]
+        row = lax.broadcasted_iota(jnp.int32, (LANES, ROW_BLOCK), 0)
+        key = lax.broadcasted_iota(jnp.int32, (LANES, ROW_BLOCK), 1) + start
+        mask = jnp.where(key > first + row, MASKED, 0.0).astype(jnp.bfloat16)
+        kt_even[KEY_WIDTH:, cols] = mask
+        kt_odd[KEY_WIDTH:, cols] = mask
+
     for j in range(parts):
-        attend_some(early + left * j // parts, early + left * (j + 1) // parts)
+        attend_some(steps * j // (parts + 1), steps * (j + 1) // (parts + 1))
         join_side(j)
+    attend_some(steps * parts // (parts + 1), steps)
     for j in range(parts):
         join_line(j)
     key_gather.finish()
@@ -401,7 +410,7 @@
             jax.ShapeDtypeStruct(q_latent.shape, bf16),
             jax.ShapeDtypeStruct(moe_tokens.shape, bf16),
         ),
-        in_specs=[vmem] * 7 + [hbm] * 3,
+        in_specs=[hbm] * 2 + [vmem] * 5 + [hbm] * 3,
         out_specs=(vmem, vmem),
         scratch_shapes=[
             pltpu.VMEM((n * queries, KEY_WIDTH), bf16),
@@ -416,7 +425,9 @@
             pltpu.VMEM((width, f_dev), bf16),
             pltpu.VMEM((width, f_dev), bf16),
             pltpu.VMEM((f_dev, width), bf16),
-            dma((3,)),
+            pltpu.VMEM(q_latent.shape, bf16),
+            pltpu.VMEM((queries, q_latent.shape[1] // LATENT * ROPE_DIM), bf16),
+            dma((5,)),
             dma((n - 1,)),
             dma((n,)),
             dma((n - 1,)),
@@ -434,7 +445,18 @@
         cost_estimate=pl.CostEstimate(
             flops=2 * 4096 * 1024 * 768, bytes_accessed=30_000_000, transcendentals=4096 * 1024
         ),
-    )(q_latent, q_rope, latents, k_rope, moe_tokens, routes, route_weights, w_gate, w_up, w_down)
+    )(
+        q_latent,
+        q_rope,
+        latents,
+        k_rope,
+        moe_tokens,
+        routes.T,
+        route_weights.T,
+        w_gate,
+        w_up,
+        w_down,
+    )
 
 
 def solution(mesh):

time: 64.7 us -> 58.2 us (0.90)
  Pallas kernels: 56.5 us -> 52.8 us
  local copies, waits for them, and re-layouts: 7.31 us -> 4.6 us
    pallas_call x1, Pallas kernels: 56.5 us -> 52.8 us  [per_device(): pl.pallas_call(functools.partial(kernel, n, n // EXPERTS), out_shape=(jax...]
    unnamed x4 -> x2, local copies, waits for them, and re-layouts: 7.31 us -> 4.6 us
where the time goes in v2:
time: 58.2 us; the launch traced here: 58 us
  Pallas kernels  52.8 us (91%)
  local copies, waits for them, and re-layouts  4.6 us (8%)
  between operations  0.64 us (1%)
    pallas_call x1, Pallas kernels, per_device(): pl.pallas_call(functools.partial(kernel, n, n // EXPERTS), out_shape=(jax...  52.8 us
    unnamed x2, local copies, waits for them, and re-layouts  4.6 us

profile of v2, /device:TPU:0, one launch (start us, length us, event | category | flops | bytes accessed | tf_op | source)
XLA Modules:
  0.0 58.0 jit_solution(5944240530658215265)
XLA Ops:
  0.6 52.8 %shard_map.113 = (bf16[64,16384]{1,0:T(8,128)(2,1)}, bf16[16,3584]{1,0:T(8,128)(2,1)}) custom-call(bf16[64,16384]{1,0:T(8,128)(2,1)} %q_lat_hbm.1, bf16[64,4096]{1,0:T(8,128)(2,1)} %q_rope_hbm.1, bf16[64,256]{1,0:T(8,128)(2,1)} %latents.1, bf16[64,64]{1,0:T(8,128)(2,1)} %k_rope.1, bf16[16,3584]{1,0:T(8,128)(2,1)} %tokens.1, s32[8,16]{1,0:T(8,128)} %bitcast.2, ...), custom_call_target="tpu_custom_call" | custom-call | flops 6442450944 | bytes 30000000 | tf_op jit(solution)/shard_map/pallas_call | solution.py:407
  53.5 3.0 %copy.14 = bf16[64,16384]{1,0:T(8,128)(2,1)} copy(bf16[64,16384]{1,0:T(8,128)(2,1)} %get-tuple-element.4) | data formatting | bytes 4194304
  56.5 1.6 %copy.15 = bf16[16,3584]{1,0:T(8,128)(2,1)} copy(bf16[16,3584]{1,0:T(8,128)(2,1)} %get-tuple-element.5) | data formatting | bytes 229376
